TPU v7x, 32 devices: a whole 2x2x4 slice. The times are simulated.
32 devices in a mesh: dp: 8 (over y, x, core), tensor: 4 (over z).
Axes of the slice: x: 2, y: 2, z: 4, core: 2. Of those that a mesh axis runs over, the one named last changes fastest.
Arguments:
- layer_input: bfloat16 [8192, 1024], P(('dp', 'tensor')), may hold values from -6 to 6
- query_weight: bfloat16 [1024, 1024], P('dp', 'tensor'), may hold values from -0.1875 to 0.1875
- key_weight: bfloat16 [1024, 1024], P('dp', 'tensor'), may hold values from -0.1875 to 0.1875
- value_weight: bfloat16 [1024, 1024], P('dp', 'tensor'), may hold values from -0.1875 to 0.1875
- mixing_weight: bfloat16 [1024, 1024], P('tensor', 'dp'), may hold values from -1.5 to 1.5
- expand_weight: bfloat16 [1024, 4096], P('dp', 'tensor'), may hold values from -0.1875 to 0.1875
- shrink_weight: bfloat16 [4096, 1024], P('tensor', 'dp'), may hold values from -0.09375 to 0.09375
- query_offset: bfloat16 [1024], P('tensor'), may hold values from -3 to 3
- value_offset: bfloat16 [1024], P('tensor'), may hold values from -3 to 3
- mixing_offset: bfloat16 [1024], replicated, may hold values from -2 to 2
- expand_offset: bfloat16 [4096], P('tensor'), may hold values from -3 to 3
- shrink_offset: bfloat16 [1024], replicated, may hold values from -2 to 2
- first_gain: bfloat16 [1024], replicated, may hold values from 0.25 to 1.75
- first_shift: bfloat16 [1024], replicated, may hold values from -2 to 2
- second_gain: bfloat16 [1024], replicated, may hold values from 0.25 to 1.75
- second_shift: bfloat16 [1024], replicated, may hold values from -2 to 2
- cotangent: bfloat16 [8192, 1024], P(('dp', 'tensor')), may hold values from -6 to 6
Outputs:
- layer_output: bfloat16 [8192, 1024], P(('dp', 'tensor'))
- input_grad: float32 [8192, 1024], P(('dp', 'tensor'))
- query_grad: float32 [1024, 1024], P('dp', 'tensor')
- key_grad: float32 [1024, 1024], P('dp', 'tensor')
- value_grad: float32 [1024, 1024], P('dp', 'tensor')
- mixing_grad: float32 [1024, 1024], P('tensor', 'dp')
- expand_grad: float32 [1024, 4096], P('dp', 'tensor')
- shrink_grad: float32 [4096, 1024], P('tensor', 'dp')
- offset_query: float32 [1024], P('tensor')
- offset_value: float32 [1024], P('tensor')
- offset_mixing: float32 [1024], replicated
- offset_expand: float32 [4096], P('tensor')
- offset_shrink: float32 [1024], replicated
- gain_first: float32 [1024], replicated
- shift_first: float32 [1024], replicated
- gain_second: float32 [1024], replicated
- shift_second: float32 [1024], replicated
All inputs are finite; a program needn't handle non-finite values.
Results may differ from a plain program's by a relative error of at most 0.015.
Values may be sent and summed in bfloat16 or wider, within the bound.
A program may use at most 128 MiB of HBM per device.

v0:
```python
import jax
import jax.numpy as jnp
from jax import lax
from jax.sharding import PartitionSpec as P

HD = 64
EPSILON = 1e-05
CONTRACT_ROWS = (((0,), (0,)), ((), ()))
CONTRACT_LAST = (((1,), (1,)), ((), ()))


def layer_norm(inputs, gain, shift):
    centered = inputs - jnp.mean(inputs, axis=-1, keepdims=True)
    variance = jnp.mean(centered * centered, axis=-1, keepdims=True)
    return centered * lax.rsqrt(variance + EPSILON) * gain + shift


def product(left, right):
    return jnp.dot(left, right, preferred_element_type=jnp.float32)


def product_rows(left, right):
    return lax.dot_general(left, right, CONTRACT_ROWS, preferred_element_type=jnp.float32)


def product_last(left, right):
    return lax.dot_general(left, right, CONTRACT_LAST, preferred_element_type=jnp.float32)


def gelu_exact(argument):
    return jax.nn.gelu(argument, approximate=False)


def attend_forward(queries, key_rows, values, block_rows):
    length, heads_here, head_size = queries.shape
    block_count = length // block_rows

    def one_block(query_block):
        scores = jnp.einsum(
            "qhd,khd->hqk", query_block, key_rows, preferred_element_type=jnp.float32
        )
        largest = jnp.max(scores, axis=-1, keepdims=True)
        weights = jnp.exp(scores - largest)
        exp_total = jnp.sum(weights, axis=-1, keepdims=True)
        probs_low = (weights / exp_total).astype(jnp.bfloat16)
        mixture = jnp.einsum("hqk,khd->qhd", probs_low, values, preferred_element_type=jnp.float32)
        log_total = (largest + jnp.log(exp_total))[..., 0]
        return (mixture.astype(jnp.bfloat16), log_total)

    mixture, log_totals = lax.map(
        one_block, queries.reshape(block_count, block_rows, heads_here, head_size)
    )
    return (mixture.reshape(length, heads_here * head_size), log_totals)


def attend_backward(queries, key_rows, values, mixture_low, log_totals, block_rows):
    length, heads_here, head_size = queries.shape
    block_count = length // block_rows

    def one_block(accumulated, inputs):
        key_sum, value_sum = accumulated
        query_block, grad_block, log_block = inputs
        scores = jnp.einsum(
            "qhd,khd->hqk", query_block, key_rows, preferred_element_type=jnp.float32
        )
        probability = jnp.exp(scores - log_block[..., None])
        probs_low = probability.astype(jnp.bfloat16)
        value_sum = value_sum + jnp.einsum(
            "hqk,qhd->khd", probs_low, grad_block, preferred_element_type=jnp.float32
        )
        prob_grad = jnp.einsum(
            "qhd,khd->hqk", grad_block, values, preferred_element_type=jnp.float32
        )
        inner_sum = jnp.sum(prob_grad * probability, axis=-1, keepdims=True)
        score_low = (probability * (prob_grad - inner_sum)).astype(jnp.bfloat16)
        query_low = jnp.einsum(
            "hqk,khd->qhd", score_low, key_rows, preferred_element_type=jnp.float32
        )
        key_sum = key_sum + jnp.einsum(
            "hqk,qhd->khd", score_low, query_block, preferred_element_type=jnp.float32
        )
        return ((key_sum, value_sum), query_low.astype(jnp.bfloat16))

    zeros = jnp.zeros((length, heads_here, head_size), jnp.float32)
    blocked = (length // block_count, heads_here, head_size)
    (key_sum, value_sum), query_low = lax.scan(
        one_block,
        (zeros, zeros),
        (
            queries.reshape((block_count,) + blocked),
            mixture_low.reshape((block_count,) + blocked),
            log_totals,
        ),
    )
    width_here = heads_here * head_size
    return (
        query_low.reshape(length, width_here),
        key_sum.astype(jnp.bfloat16).reshape(length, width_here),
        value_sum.astype(jnp.bfloat16).reshape(length, width_here),
    )


def body(
    layer_input,
    query_weight,
    key_weight,
    value_weight,
    mixing_weight,
    expand_weight,
    shrink_weight,
    query_offset,
    value_offset,
    mixing_offset,
    expand_offset,
    shrink_offset,
    first_gain,
    first_shift,
    second_gain,
    second_shift,
    cotangent,
):
    local_rows = layer_input.shape[0]
    tensor_size = lax.axis_size("tensor")
    length = local_rows * tensor_size
    block_rows = min(512, length)
    heads_here = query_weight.shape[1] // HD
    scaling = HD ** (-0.5)
    head_shape = (length, heads_here, HD)
    gathered = (
        lax.all_gather(query_weight, "dp", axis=0, tiled=True),
        lax.all_gather(key_weight, "dp", axis=0, tiled=True),
        lax.all_gather(value_weight, "dp", axis=0, tiled=True),
        lax.all_gather(mixing_weight, "dp", axis=1, tiled=True),
        lax.all_gather(expand_weight, "dp", axis=0, tiled=True),
        lax.all_gather(shrink_weight, "dp", axis=1, tiled=True),
    )
    query_full, key_full, value_full, mixing_full, expand_full, shrink_full = gathered
    sequence = lax.all_gather(layer_input, "tensor", axis=0, tiled=True)
    queries = ((product(sequence, query_full) + query_offset.astype(jnp.float32)) * scaling).astype(
        jnp.bfloat16
    )
    key_rows = product(sequence, key_full).astype(jnp.bfloat16)
    values = (product(sequence, value_full) + value_offset.astype(jnp.float32)).astype(jnp.bfloat16)
    mixture, log_totals = attend_forward(
        queries.reshape(head_shape),
        key_rows.reshape(head_shape),
        values.reshape(head_shape),
        block_rows,
    )
    attended_part = lax.psum_scatter(
        product(mixture, mixing_full).astype(jnp.bfloat16),
        "tensor",
        scatter_dimension=0,
        tiled=True,
    )
    attended = layer_input.astype(jnp.float32) + attended_part + mixing_offset.astype(jnp.float32)
    first_norm, first_back = jax.vjp(
        layer_norm, attended, first_gain.astype(jnp.float32), first_shift.astype(jnp.float32)
    )
    normed = lax.all_gather(first_norm.astype(jnp.bfloat16), "tensor", axis=0, tiled=True)
    expanded = product(normed, expand_full) + expand_offset.astype(jnp.float32)
    hidden_act, gelu_back = jax.vjp(gelu_exact, expanded)
    hidden = hidden_act.astype(jnp.bfloat16)
    shrunk = lax.psum_scatter(
        product(hidden, shrink_full).astype(jnp.bfloat16), "tensor", scatter_dimension=0, tiled=True
    )
    summed = first_norm + shrunk + shrink_offset.astype(jnp.float32)
    normalized, second_back = jax.vjp(
        layer_norm, summed, second_gain.astype(jnp.float32), second_shift.astype(jnp.float32)
    )
    summed_grad, gain_second, shift_second = second_back(cotangent.astype(jnp.float32))
    query_back, key_back, value_back, mixing_back, expand_back, shrink_back = gathered
    branch_rows = lax.all_gather(summed_grad.astype(jnp.bfloat16), "tensor", axis=0, tiled=True)
    shrink_local = product_rows(hidden, branch_rows)
    hidden_grad = product_last(branch_rows, shrink_back)
    expanded_low = gelu_back(hidden_grad)[0].astype(jnp.bfloat16)
    expand_sum = jnp.sum(expanded_low.astype(jnp.float32), axis=0)
    expand_local = product_rows(normed, expanded_low)
    first_grad = (
        lax.psum_scatter(
            product_last(expanded_low, expand_back).astype(jnp.bfloat16),
            "tensor",
            scatter_dimension=0,
            tiled=True,
        )
        + summed_grad
    )
    shrink_sum = jnp.sum(summed_grad, axis=0)
    attended_grad, gain_first, shift_first = first_back(first_grad)
    mixing_sum = jnp.sum(attended_grad, axis=0)
    attended_rows = lax.all_gather(attended_grad.astype(jnp.bfloat16), "tensor", axis=0, tiled=True)
    mixing_local = product_rows(mixture, attended_rows)
    mixture_low = product_last(attended_rows, mixing_back).astype(jnp.bfloat16)
    query_low, key_low, value_low = attend_backward(
        queries.reshape(head_shape),
        key_rows.reshape(head_shape),
        values.reshape(head_shape),
        mixture_low,
        log_totals,
        block_rows,
    )
    query_local = product_rows(sequence, query_low) * scaling
    key_local = product_rows(sequence, key_low)
    value_local = product_rows(sequence, value_low)
    query_sum = jnp.sum(query_low.astype(jnp.float32), axis=0) * scaling
    value_sum = jnp.sum(value_low.astype(jnp.float32), axis=0)
    input_grad = (
        lax.psum_scatter(
            (
                product_last(query_low, query_back) * scaling
                + product_last(key_low, key_back)
                + product_last(value_low, value_back)
            ).astype(jnp.bfloat16),
            "tensor",
            scatter_dimension=0,
            tiled=True,
        ).astype(jnp.float32)
        + attended_grad
    )
    query_grad, key_grad, value_grad, mixing_grad, expand_grad, shrink_grad = (
        lax.psum_scatter(
            query_local.astype(jnp.bfloat16), "dp", scatter_dimension=0, tiled=True
        ).astype(jnp.float32),
        lax.psum_scatter(
            key_local.astype(jnp.bfloat16), "dp", scatter_dimension=0, tiled=True
        ).astype(jnp.float32),
        lax.psum_scatter(
            value_local.astype(jnp.bfloat16), "dp", scatter_dimension=0, tiled=True
        ).astype(jnp.float32),
        lax.psum_scatter(
            mixing_local.astype(jnp.bfloat16), "dp", scatter_dimension=1, tiled=True
        ).astype(jnp.float32),
        lax.psum_scatter(
            expand_local.astype(jnp.bfloat16), "dp", scatter_dimension=0, tiled=True
        ).astype(jnp.float32),
        lax.psum_scatter(
            shrink_local.astype(jnp.bfloat16), "dp", scatter_dimension=1, tiled=True
        ).astype(jnp.float32),
    )
    tensor_index = lax.axis_index("tensor")
    selector = (jnp.arange(tensor_size)[:, None] == tensor_index).astype(jnp.float32)

    def spread_out(vector):
        return (selector * vector[None, :]).reshape(-1)

    totals = lax.psum(
        (
            gain_first,
            shift_first,
            gain_second,
            shift_second,
            mixing_sum,
            shrink_sum,
            spread_out(query_sum),
            spread_out(value_sum),
            spread_out(expand_sum),
        ),
        ("dp", "tensor"),
    )

    def own_slice(full_vector, slice_size):
        return lax.dynamic_slice_in_dim(full_vector, tensor_index * slice_size, slice_size, 0)

    offset_query = own_slice(totals[6], query_sum.shape[0])
    offset_value = own_slice(totals[7], value_sum.shape[0])
    offset_expand = own_slice(totals[8], expand_sum.shape[0])
    return (
        normalized.astype(jnp.bfloat16),
        input_grad,
        query_grad,
        key_grad,
        value_grad,
        mixing_grad,
        expand_grad,
        shrink_grad,
        offset_query,
        offset_value,
        totals[4],
        offset_expand,
        totals[5],
        totals[0],
        totals[1],
        totals[2],
        totals[3],
    )


def solution(mesh):
    placed = (
        P(("dp", "tensor"), None),
        P("dp", "tensor"),
        P("dp", "tensor"),
        P("dp", "tensor"),
        P("tensor", "dp"),
        P("dp", "tensor"),
        P("tensor", "dp"),
        P("tensor"),
        P("tensor"),
        P(),
        P("tensor"),
        P(),
        P(),
        P(),
        P(),
        P(),
        P(("dp", "tensor"), None),
    )
    return jax.shard_map(
        body,
        mesh=mesh,
        in_specs=placed,
        out_specs=(
            P(("dp", "tensor"), None),
            P(("dp", "tensor"), None),
            P("dp", "tensor"),
            P("dp", "tensor"),
            P("dp", "tensor"),
            P("tensor", "dp"),
            P("dp", "tensor"),
            P("tensor", "dp"),
            P("tensor"),
            P("tensor"),
            P(),
            P("tensor"),
            P(),
            P(),
            P(),
            P(),
            P(),
        ),
        check_vma=False,
    )
```

profile of v0, /device:TPU:0, one launch (start us, length us, event | category | flops | bytes accessed | tf_op | source)
XLA Modules:
  0.0 704.7 jit_solution(7860083018517622834)
XLA Ops:
  10.1 11.6 %all_gather.31 = bf16[1024,256]{1,0:T(8,128)(2,1)S(1)} all-gather(bf16[128,256]{1,0:T(8,128)(2,1)} %param.22), channel_id=1, replica_groups=mesh['dp'=8,'tensor'=4] {'dp'}, dimensions={0}, use_global_device_ids=true | all-gather | bytes 589824 | tf_op jit(solution)/shard_map/all_gather | solution.py:130
  21.7 9.5 %all_gather.32 = bf16[1024,256]{1,0:T(8,128)(2,1)S(1)} all-gather(bf16[128,256]{1,0:T(8,128)(2,1)} %param.23), channel_id=1, replica_groups=mesh['dp'=8,'tensor'=4] {'dp'}, dimensions={0}, use_global_device_ids=true | all-gather | bytes 589824 | tf_op jit(solution)/shard_map/all_gather | solution.py:131
  31.3 9.2 %all_gather.33 = bf16[1024,256]{1,0:T(8,128)(2,1)S(1)} all-gather(bf16[128,256]{1,0:T(8,128)(2,1)} %param.24), channel_id=1, replica_groups=mesh['dp'=8,'tensor'=4] {'dp'}, dimensions={0}, use_global_device_ids=true | all-gather | bytes 589824 | tf_op jit(solution)/shard_map/all_gather | solution.py:132
  40.4 10.9 %all_gather.34 = bf16[256,1024]{1,0:T(8,128)(2,1)} all-gather(bf16[256,128]{1,0:T(8,128)(2,1)} %param.25), channel_id=1, replica_groups=mesh['dp'=8,'tensor'=4] {'dp'}, dimensions={1}, use_global_device_ids=true | all-gather | bytes 589824 | tf_op jit(solution)/shard_map/all_gather | solution.py:133
  51.3 7.8 %all-gather.7.cloned.1.call-done = bf16[1024,1024]{1,0:T(8,128)(2,1)} async-done(((bf16[256,1024]{1,0:T(8,128)(2,1)}), bf16[1024,1024]{1,0:T(8,128)(2,1)}) %all-gather.7.cloned.1.call-update) | async-done | bytes 2097168 | tf_op jit(solution)/shard_map/all_gather | solution.py:138
  68.0 12.4 %while.27 = (s32[]{:T(128)}, bf16[2,512,4,64]{1,3,2,0:T(8,128)(2,1)S(1)}, f32[2,4,512]{2,1,0:T(4,128)S(1)}, bf16[2,512,4,64]{1,3,2,0:T(8,128)(2,1)S(1)}, bf16[10...) while((s32[]{:T(128)}, bf16[2,512,4,64]{1,3,2,0:T(8,128)(2,1)S(1)}, ...), condition=%wide.region_3.4_spmd, body=%wide.region_0.3_spmd.sunk | while | flops 549582848 | bytes 26804320 | solution.py:50
  83.9 42.1 %reduce-scatter.21.cloned.1.call-done = bf16[256,1024]{1,0:T(8,128)(2,1)} async-done(((bf16[1024,1024]{1,0:T(8,128)(2,1)}), bf16[256,1024]{1,0:T(8,128)(2,1)}) %reduce-scatter.21.cloned.1.call-update) | async-done | bytes 524304 | tf_op jit(solution)/shard_map/reduce_scatter | solution.py:150
  132.0 43.8 %all-gather.9.cloned.1.call-done = bf16[1024,1024]{1,0:T(8,128)(2,1)} async-done(((bf16[256,1024]{1,0:T(8,128)(2,1)}), bf16[1024,1024]{1,0:T(8,128)(2,1)}) %all-gather.9.cloned.1.call-update) | async-done | bytes 2097168 | tf_op jit(solution)/shard_map/all_gather | solution.py:160
  175.8 14.9 %multiply_convert_fusion.1 = (bf16[1024,1024]{1,0:T(8,128)(2,1)}, f32[1024,1024]{1,0:T(8,128)}, f32[1024,1024]{1,0:T(8,128)}) fusion(f32[1024]{0:T(1024)S(1)} %convert_element_type.190, bf16[1024,1024]{1,0:T(8,128)(2,1)} %all-gather.9.cloned.1.call-done, bf16[1024,1024]{1,0:T(8,128)(2,1)} %all-gather.11.cloned.1.call-done), kind=kOutput, calls=%fused_computation.45 | convolution fusion | flops 2216689664 | bytes 14684160 | tf_op jit(solution)/shard_map/dot_general | solution.py:19
  190.6 13.9 %all-gather.13.cloned.1.call-done = bf16[1024,1024]{1,0:T(8,128)(2,1)} async-done(((bf16[1024,128]{1,0:T(8,128)(2,1)}), bf16[1024,1024]{1,0:T(8,128)(2,1)}) %all-gather.13.cloned.1.call-update) | async-done | bytes 2097168 | tf_op jit(solution)/shard_map/all_gather | solution.py:135
  204.5 6.0 convolution_convert_fusion.4
  210.6 43.9 %reduce-scatter.23.cloned.1.call-done = bf16[256,1024]{1,0:T(8,128)(2,1)} async-done(((bf16[1024,1024]{1,0:T(8,128)(2,1)}), bf16[256,1024]{1,0:T(8,128)(2,1)}) %reduce-scatter.23.cloned.1.call-update) | async-done | bytes 524304 | tf_op jit(solution)/shard_map/reduce_scatter | solution.py:164
  260.3 44.8 %all-gather.15.cloned.1.call-done = bf16[1024,1024]{1,0:T(8,128)(2,1)} async-done(((bf16[256,1024]{1,0:T(8,128)(2,1)}), bf16[1024,1024]{1,0:T(8,128)(2,1)}) %all-gather.15.cloned.1.call-update) | async-done | bytes 2097168 | tf_op jit(solution)/shard_map/all_gather | solution.py:173
  305.1 8.5 %convert_reduce_fusion = (f32[1024]{0:T(1024)S(1)}, bf16[1024,1024]{1,0:T(8,128)(2,1)S(1)}) fusion(f32[1024,1024]{1,0:T(8,128)} %get-tuple-element.287, f32[1024,1024]{1,0:T(8,128)} %get-tuple-element.297, f32[1024]{0:T(1024)S(1)} %convert_element_type.190, bf16[1024,1024]{1,0:T(8,128)(2,1)} %all-gather.15.cloned.1.call-done, ...), kind=kOutput, calls=%fused_computation.42 | convolution fusion | flops 2165308416 | bytes 14688256 | tf_op jit(solution)/shard_map/dot_general | solution.py:27
  318.7 42.8 %reduce-scatter.25.cloned.1.call-done = bf16[256,1024]{1,0:T(8,128)(2,1)} async-done(((bf16[1024,1024]{1,0:T(8,128)(2,1)}), bf16[256,1024]{1,0:T(8,128)(2,1)}) %reduce-scatter.25.cloned.1.call-update) | async-done | bytes 524304 | tf_op jit(solution)/shard_map/reduce_scatter | solution.py:180
  374.2 6.1 convolution_convert_fusion.2
  380.6 31.3 %all-gather.17.cloned.1.call-done = bf16[1024,1024]{1,0:T(8,128)(2,1)} async-done(((bf16[256,1024]{1,0:T(8,128)(2,1)}), bf16[1024,1024]{1,0:T(8,128)(2,1)}) %all-gather.17.cloned.1.call-update) | async-done | bytes 2097168 | tf_op jit(solution)/shard_map/all_gather | solution.py:191
  426.4 21.4 %while.28 = (s32[]{:T(128)}, f32[1024,4,64]{0,2,1:T(8,128)S(1)}, f32[1024,4,64]{0,2,1:T(8,128)S(1)}, bf16[2,512,4,64]{1,3,2,0:T(8,128)(2,1)}, bf16[2,512,4,64]{1...) while((s32[]{:T(128)}, f32[1024,4,64]{0,2,1:T(8,128)S(1)}, ...), condition=%wide.region_17.18_spmd.clone, body=%wide.region_15.17_spmd.clone.sunk | while | flops 1362229248 | bytes 76341480 | solution.py:86
  469.8 29.9 %reduce-scatter.29.cloned.1.call-done = bf16[128,1024]{1,0:T(8,128)(2,1)} async-done(((bf16[1024,1024]{1,0:T(8,128)(2,1)}), bf16[128,1024]{1,0:T(8,128)(2,1)}) %reduce-scatter.29.cloned.1.call-update) | async-done | bytes 262160 | tf_op jit(solution)/shard_map/reduce_scatter | solution.py:233
  502.0 40.7 %all-reduce = (f32[1024]{0:T(1024)S(1)}, f32[1024]{0:T(1024)S(1)}, f32[1024]{0:T(1024)}, f32[4096]{0:T(1024)S(1)}, f32[1024]{0:T(1024)}, /*index=5*/f32[1024]{0:...) all-reduce(f32[1024]{0:T(1024)S(1)} %bitcast.175, ...), channel_id=1, replica_groups=mesh['dp'=8,'tensor'=4] {'dp','tensor'}, use_global_device_ids=true, to_apply=%region_26.27 | all-reduce | flops 12288 | bytes 98304 | tf_op jit(solution)/shard_map/psum | solution.py:246
  546.2 28.1 %reduce-scatter.31.cloned.1.call-done = bf16[128,256]{1,0:T(8,128)(2,1)} async-done(((bf16[1024,256]{1,0:T(8,128)(2,1)}), bf16[128,256]{1,0:T(8,128)(2,1)}) %reduce-scatter.31.cloned.1.call-update) | async-done | bytes 65552
  576.1 35.8 %reduce-scatter.33.cloned.1.call-done = bf16[128,256]{1,0:T(8,128)(2,1)} async-done(((bf16[1024,256]{1,0:T(8,128)(2,1)}), bf16[128,256]{1,0:T(8,128)(2,1)}) %reduce-scatter.33.cloned.1.call-update) | async-done | bytes 65552
  613.6 35.4 %reduce-scatter.35.cloned.1.call-done = bf16[128,256]{1,0:T(8,128)(2,1)} async-done(((bf16[1024,256]{1,0:T(8,128)(2,1)}), bf16[128,256]{1,0:T(8,128)(2,1)}) %reduce-scatter.35.cloned.1.call-update) | async-done | bytes 65552
  650.7 44.2 %reduce-scatter.27.cloned.1.call-done = bf16[256,1024]{1,0:T(8,128)(2,1)} async-done(((bf16[1024,1024]{1,0:T(8,128)(2,1)}), bf16[256,1024]{1,0:T(8,128)(2,1)}) %reduce-scatter.27.cloned.1.call-update) | async-done | bytes 524304 | tf_op jit(solution)/shard_map/reduce_scatter | solution.py:208
  (208 shorter events, 127.0 us)
Async XLA Ops:
  8.0 51.1 %all-gather.7.cloned.1.call-start = ((), (), s32[]{:S(2)}) async-start(), calls=%async_computation.10 | async-start | bytes 2621440 | tf_op jit(solution)/shard_map/all_gather | solution.py:138
  8.8 117.2 %reduce-scatter.21.cloned.1.call-start = ((), (), s32[]{:S(2)}) async-start(), calls=%async_computation.11 | async-start | bytes 2621440 | tf_op jit(solution)/shard_map/reduce_scatter | solution.py:150
  21.7 39.7 %copy-start.11 = (bf16[1024,256]{1,0:T(8,128)(2,1)}, bf16[1024,256]{1,0:T(8,128)(2,1)S(1)}, u32[]{:S(2)}) copy-start(bf16[1024,256]{1,0:T(8,128)(2,1)S(1)} %all_gather.31) | copy-start | bytes 1572868
  80.4 45.5 %copy-start = (bf16[256,1024]{1,0:T(8,128)(2,1)S(1)}, bf16[256,1024]{1,0:T(8,128)(2,1)}, u32[]{:S(2)}) copy-start(bf16[256,1024]{1,0:T(8,128)(2,1)} %param.21) | copy-start | bytes 1572868
  81.1 49.7 %copy-start.19 = (bf16[32,8,2,512]{3,1,2,0:T(8,128)(2,1)}, bf16[32,8,2,512]{3,1,2,0:T(8,128)(2,1)S(1)}, u32[]{:S(2)}) copy-start(bf16[32,8,2,512]{3,1,2,0:T(8,128)(2,1)S(1)} %copy.74) | copy-start | bytes 1572868
  83.1 48.8 %copy-start.23 = (bf16[1024]{0:T(1024)(128)(2,1)S(1)}, bf16[1024]{0:T(1024)(128)(2,1)}, u32[]{:S(2)}) copy-start(bf16[1024]{0:T(1024)(128)(2,1)} %param.31) | copy-start | bytes 6148
  83.2 48.8 %all-gather.11.cloned.1.call-start = ((), (), s32[]{:S(2)}) async-start(), calls=%async_computation.13 | async-start | bytes 2359296 | tf_op jit(solution)/shard_map/all_gather | solution.py:134
  83.8 92.0 %all-gather.9.cloned.1.call-start = ((), (), s32[]{:S(2)}) async-start(), calls=%async_computation.12 | async-start | bytes 2621440 | tf_op jit(solution)/shard_map/all_gather | solution.py:160
  130.8 73.7 %all-gather.13.cloned.1.call-start = ((), (), s32[]{:S(2)}) async-start(), calls=%async_computation.14 | async-start | bytes 2359296 | tf_op jit(solution)/shard_map/all_gather | solution.py:135
  131.4 123.2 %reduce-scatter.23.cloned.1.call-start = ((), (), s32[]{:S(2)}) async-start(), calls=%async_computation.15 | async-start | bytes 2621440 | tf_op jit(solution)/shard_map/reduce_scatter | solution.py:164
  204.5 50.0 %copy-start.2 = (bf16[256,1024]{1,0:T(8,128)(2,1)S(1)}, bf16[256,1024]{1,0:T(8,128)(2,1)}, u32[]{:S(2)}) copy-start(bf16[256,1024]{1,0:T(8,128)(2,1)} %reduce-scatter.21.cloned.1.call-done) | copy-start | bytes 1572868
  210.5 45.9 %copy-start.17 = (bf16[256,1024]{1,0:T(8,128)(2,1)S(1)}, bf16[256,1024]{1,0:T(8,128)(2,1)}, u32[]{:S(2)}) copy-start(bf16[256,1024]{1,0:T(8,128)(2,1)} %param.37) | copy-start | bytes 1572868
  210.5 94.6 %all-gather.15.cloned.1.call-start = ((), (), s32[]{:S(2)}) async-start(), calls=%async_computation.16 | async-start | bytes 2621440 | tf_op jit(solution)/shard_map/all_gather | solution.py:173
  260.1 101.4 %reduce-scatter.25.cloned.1.call-start = ((), (), s32[]{:S(2)}) async-start(), calls=%async_computation.17 | async-start | bytes 2621440 | tf_op jit(solution)/shard_map/reduce_scatter | solution.py:180
  318.7 93.2 %all-gather.17.cloned.1.call-start = ((), (), s32[]{:S(2)}) async-start(), calls=%async_computation.18 | async-start | bytes 2621440 | tf_op jit(solution)/shard_map/all_gather | solution.py:191
  366.9 100.9 %reduce-scatter.39.cloned.1.call-start = ((), (), s32[]{:S(2)}) async-start(), calls=%async_computation.25 | async-start | bytes 2359296
  374.2 125.6 %reduce-scatter.29.cloned.1.call-start = ((), (), s32[]{:S(2)}) async-start(), calls=%async_computation.20 | async-start | bytes 2359296 | tf_op jit(solution)/shard_map/reduce_scatter | solution.py:233
  380.3 164.2 %reduce-scatter.37.cloned.1.call-start = ((), (), s32[]{:S(2)}) async-start(), calls=%async_computation.24 | async-start | bytes 589824
  425.6 148.8 %reduce-scatter.31.cloned.1.call-start = ((), (), s32[]{:S(2)}) async-start(), calls=%async_computation.21 | async-start | bytes 589824
  453.0 158.9 %reduce-scatter.33.cloned.1.call-start = ((), (), s32[]{:S(2)}) async-start(), calls=%async_computation.22 | async-start | bytes 589824
  456.5 192.5 %reduce-scatter.35.cloned.1.call-start = ((), (), s32[]{:S(2)}) async-start(), calls=%async_computation.23 | async-start | bytes 589824
  462.8 232.1 %reduce-scatter.27.cloned.1.call-start = ((), (), s32[]{:S(2)}) async-start(), calls=%async_computation.19 | async-start | bytes 2621440 | tf_op jit(solution)/shard_map/reduce_scatter | solution.py:208
  467.6 33.9 %copy-start.8 = (bf16[2,512,4,64]{1,3,2,0:T(8,128)(2,1)S(1)}, bf16[2,512,4,64]{1,3,2,0:T(8,128)(2,1)}, u32[]{:S(2)}) copy-start(bf16[2,512,4,64]{1,3,2,0:T(8,128)(2,1)} %get-tuple-element.101) | copy-start | bytes 1572868
  467.6 227.3 %copy-start.5 = (f32[256,1024]{1,0:T(8,128)S(1)}, f32[256,1024]{1,0:T(8,128)}, u32[]{:S(2)}) copy-start(f32[256,1024]{1,0:T(8,128)} %copy-done.4) | copy-start | bytes 3145732
  (24 other events, 140.1 us)
Sparse Core Ops, SparseCore 0:
  10.4 48.6 all-gather.6
  83.3 42.5 reduce-scatter.20
  210.6 43.8 reduce-scatter.22
  318.8 42.6 reduce-scatter.24
Sparse Core Ops, SparseCore 1:
  85.7 26.4 all-gather.10
  130.9 44.8 all-gather.8
  177.7 26.8 all-gather.12
  260.2 44.8 all-gather.14
  367.0 44.9 all-gather.16
  415.6 39.9 reduce-scatter.38
  458.7 41.1 reduce-scatter.28
  503.0 34.1 reduce-scatter.36
  540.1 34.1 reduce-scatter.30
  577.7 34.1 reduce-scatter.32
  614.9 34.1 reduce-scatter.34
  651.4 43.5 reduce-scatter.26
where the time goes:
time: 714 us; the launch traced here: 705 us
  waiting for transfers between devices  446 us (62%)
  matrix products  99.1 us (14%)
  blocking collectives  81.9 us (11%)
  local copies, waits for them, and re-layouts  30.4 us (4%)
  other arithmetic  29.1 us (4%)
  between operations  16.4 us (2%)
    unnamed x21, waiting for transfers between devices  101 us
    all_gather x1, waiting for transfers between devices, body(): lax.all_gather(summed_grad.astype(jnp.bfloat16), 'tensor', axis=0, tiled=...  44.8 us
    reduce_scatter x1, waiting for transfers between devices, body(): lax.psum_scatter((product_last(query_low, query_back) * scaling + product...  44.2 us
    reduce_scatter x1, waiting for transfers between devices, body(): lax.psum_scatter(product(hidden, shrink_full).astype(jnp.bfloat16), 'tens...  43.9 us
    all_gather x1, waiting for transfers between devices, body(): lax.all_gather(first_norm.astype(jnp.bfloat16), 'tensor', axis=0, tiled=T...  43.8 us
    reduce_scatter x1, waiting for transfers between devices, body(): lax.psum_scatter(product_last(expanded_low, expand_back).astype(jnp.bfloa...  42.8 us
    reduce_scatter x1, waiting for transfers between devices, body(): lax.psum_scatter(product(mixture, mixing_full).astype(jnp.bfloat16), 'ten...  42.1 us
    psum x1, blocking collectives, body(): lax.psum((gain_first, shift_first, gain_second, shift_second, mixing_sum,...  40.7 us
  transfers between devices with their start and end apart: 16, of which 13 were waited for; matrix products, arithmetic and copies ran while one was open for 14% of the time, Pallas kernels for 0%

commit v1 on v0

--- a/solution.py
+++ b/solution.py
@@ -7,6 +7,20 @@
 EPSILON = 1e-05
 CONTRACT_ROWS = (((0,), (0,)), ((), ()))
 CONTRACT_LAST = (((1,), (1,)), ((), ()))
+
+
+def raise_the_row(load, join_dim):
+    w2, left_arr = (lax.axis_size("tensor"), lax.axis_index("tensor"))
+    h_now, part_next = (load, 1)
+    while part_next < w2:
+        known = lax.ppermute(
+            h_now, axis_name="tensor", perm=[(no, no ^ part_next) for no in range(w2)]
+        )
+        arr_next = jnp.concatenate([h_now, known], axis=join_dim)
+        item_now = jnp.concatenate([known, h_now], axis=join_dim)
+        h_now = jnp.where(left_arr & part_next == 0, arr_next, item_now)
+        part_next = 2 * part_next
+    return h_now
 
 
 def layer_norm(inputs, gain, shift):
@@ -188,7 +202,7 @@
     shrink_sum = jnp.sum(summed_grad, axis=0)
     attended_grad, gain_first, shift_first = first_back(first_grad)
     mixing_sum = jnp.sum(attended_grad, axis=0)
-    attended_rows = lax.all_gather(attended_grad.astype(jnp.bfloat16), "tensor", axis=0, tiled=True)
+    attended_rows = raise_the_row(attended_grad.astype(jnp.bfloat16), 0)
     mixing_local = product_rows(mixture, attended_rows)
     mixture_low = product_last(attended_rows, mixing_back).astype(jnp.bfloat16)
     query_low, key_low, value_low = attend_backward(

time: 714 us -> 665 us (0.931)
  waiting for transfers between devices: 446 us -> 391 us
    ppermute x0 -> x2, waiting for transfers between devices: none -> 59 us  [raise_the_row(): lax.ppermute(h_now, axis_name='tensor', perm=[(no, no ^ part_next) for no...]
    unnamed x21 -> x20, waiting for transfers between devices: 101 us -> 64.3 us
    all_gather x1 -> x0, waiting for transfers between devices: 31.3 us -> none  [body(): lax.all_gather(attended_grad.astype(jnp.bfloat16), 'tensor', axis=0, tile...]
    reduce_scatter x1, waiting for transfers between devices: 29.9 us -> 0.01 us  [body(): lax.psum_scatter(expand_local.astype(jnp.bfloat16), 'dp', scatter_dimensi...]
    reduce_scatter x1, waiting for transfers between devices: 42.8 us -> 26.5 us  [body(): lax.psum_scatter(product_last(expanded_low, expand_back).astype(jnp.bfloa...]
    unnamed x71 -> x75, local copies, waits for them, and re-layouts: 21.5 us -> 22.7 us
  transfers between devices with their start and end apart: 16 -> 17, of which waited for: 13 -> 12; matrix products, arithmetic and copies ran while one was open for 14% -> 17% of each run, Pallas kernels for 0% -> 0%
where the time goes in v1:
time: 665 us; the launch traced here: 656 us
  waiting for transfers between devices  391 us (59%)
  matrix products  102 us (15%)
  blocking collectives  80.8 us (12%)
  local copies, waits for them, and re-layouts  31.6 us (5%)
  other arithmetic  30.3 us (5%)
  between operations  16.7 us (3%)
    unnamed x20, waiting for transfers between devices  64.3 us
    ppermute x2, waiting for transfers between devices, raise_the_row(): lax.ppermute(h_now, axis_name='tensor', perm=[(no, no ^ part_next) for no...  59 us
    all_gather x1, waiting for transfers between devices, body(): lax.all_gather(summed_grad.astype(jnp.bfloat16), 'tensor', axis=0, tiled=...  44.7 us
    reduce_scatter x1, waiting for transfers between devices, body(): lax.psum_scatter((product_last(query_low, query_back) * scaling + product...  44.6 us
    all_gather x1, waiting for transfers between devices, body(): lax.all_gather(first_norm.astype(jnp.bfloat16), 'tensor', axis=0, tiled=T...  44.1 us
    reduce_scatter x1, waiting for transfers between devices, body(): lax.psum_scatter(product(hidden, shrink_full).astype(jnp.bfloat16), 'tens...  43.9 us
    reduce_scatter x1, waiting for transfers between devices, body(): lax.psum_scatter(product(mixture, mixing_full).astype(jnp.bfloat16), 'ten...  42.1 us
    psum x1, blocking collectives, body(): lax.psum((gain_first, shift_first, gain_second, shift_second, mixing_sum,...  39.6 us
  transfers between devices with their start and end apart: 17, of which 12 were waited for; matrix products, arithmetic and copies ran while one was open for 17% of the time, Pallas kernels for 0%

profile of v1, /device:TPU:0, one launch (start us, length us, event | category | flops | bytes accessed | tf_op | source)
XLA Modules:
  0.0 656.2 jit_solution(8691400540521905568)
XLA Ops:
  10.1 11.6 %all_gather.28 = bf16[1024,256]{1,0:T(8,128)(2,1)S(1)} all-gather(bf16[128,256]{1,0:T(8,128)(2,1)} %param.22), channel_id=1, replica_groups=mesh['dp'=8,'tensor'=4] {'dp'}, dimensions={0}, use_global_device_ids=true | all-gather | bytes 589824 | tf_op jit(solution)/shard_map/all_gather | solution.py:144
  21.7 9.5 %all_gather.29 = bf16[1024,256]{1,0:T(8,128)(2,1)S(1)} all-gather(bf16[128,256]{1,0:T(8,128)(2,1)} %param.23), channel_id=1, replica_groups=mesh['dp'=8,'tensor'=4] {'dp'}, dimensions={0}, use_global_device_ids=true | all-gather | bytes 589824 | tf_op jit(solution)/shard_map/all_gather | solution.py:145
  31.3 9.2 %all_gather.30 = bf16[1024,256]{1,0:T(8,128)(2,1)S(1)} all-gather(bf16[128,256]{1,0:T(8,128)(2,1)} %param.24), channel_id=1, replica_groups=mesh['dp'=8,'tensor'=4] {'dp'}, dimensions={0}, use_global_device_ids=true | all-gather | bytes 589824 | tf_op jit(solution)/shard_map/all_gather | solution.py:146
  40.4 10.9 %all_gather.31 = bf16[256,1024]{1,0:T(8,128)(2,1)} all-gather(bf16[256,128]{1,0:T(8,128)(2,1)} %param.25), channel_id=1, replica_groups=mesh['dp'=8,'tensor'=4] {'dp'}, dimensions={1}, use_global_device_ids=true | all-gather | bytes 589824 | tf_op jit(solution)/shard_map/all_gather | solution.py:147
  51.3 7.7 %all-gather.6.cloned.1.call-done = bf16[1024,1024]{1,0:T(8,128)(2,1)} async-done(((bf16[256,1024]{1,0:T(8,128)(2,1)}), bf16[1024,1024]{1,0:T(8,128)(2,1)}) %all-gather.6.cloned.1.call-update) | async-done | bytes 2097168 | tf_op jit(solution)/shard_map/all_gather | solution.py:152
  68.0 12.4 %while.27 = (s32[]{:T(128)}, bf16[2,512,4,64]{1,3,2,0:T(8,128)(2,1)S(1)}, f32[2,4,512]{2,1,0:T(4,128)S(1)}, bf16[2,512,4,64]{1,3,2,0:T(8,128)(2,1)S(1)}, bf16[10...) while((s32[]{:T(128)}, bf16[2,512,4,64]{1,3,2,0:T(8,128)(2,1)S(1)}, ...), condition=%wide.region_3.4_spmd, body=%wide.region_0.3_spmd.sunk | while | flops 549582848 | bytes 26804320 | solution.py:64
  83.9 42.1 %reduce-scatter.21.cloned.1.call-done = bf16[256,1024]{1,0:T(8,128)(2,1)} async-done(((bf16[1024,1024]{1,0:T(8,128)(2,1)}), bf16[256,1024]{1,0:T(8,128)(2,1)}) %reduce-scatter.21.cloned.1.call-update) | async-done | bytes 524304 | tf_op jit(solution)/shard_map/reduce_scatter | solution.py:164
  131.7 44.1 %all-gather.8.cloned.1.call-done = bf16[1024,1024]{1,0:T(8,128)(2,1)} async-done(((bf16[256,1024]{1,0:T(8,128)(2,1)}), bf16[1024,1024]{1,0:T(8,128)(2,1)}) %all-gather.8.cloned.1.call-update) | async-done | bytes 2097168 | tf_op jit(solution)/shard_map/all_gather | solution.py:174
  175.8 14.9 %multiply_convert_fusion.1 = (bf16[1024,1024]{1,0:T(8,128)(2,1)}, f32[1024,1024]{1,0:T(8,128)}, f32[1024,1024]{1,0:T(8,128)}) fusion(f32[1024]{0:T(1024)S(1)} %convert_element_type.190, bf16[1024,1024]{1,0:T(8,128)(2,1)} %all-gather.8.cloned.1.call-done, bf16[1024,1024]{1,0:T(8,128)(2,1)} %all-gather.10.cloned.1.call-done), kind=kOutput, calls=%fused_computation.45 | convolution fusion | flops 2216689664 | bytes 14684160 | tf_op jit(solution)/shard_map/dot_general | solution.py:33
  190.7 13.8 %all-gather.12.cloned.1.call-done = bf16[1024,1024]{1,0:T(8,128)(2,1)} async-done(((bf16[1024,128]{1,0:T(8,128)(2,1)}), bf16[1024,1024]{1,0:T(8,128)(2,1)}) %all-gather.12.cloned.1.call-update) | async-done | bytes 2097168 | tf_op jit(solution)/shard_map/all_gather | solution.py:149
  204.5 5.9 convolution_convert_fusion.4
  210.6 43.9 %reduce-scatter.23.cloned.1.call-done = bf16[256,1024]{1,0:T(8,128)(2,1)} async-done(((bf16[1024,1024]{1,0:T(8,128)(2,1)}), bf16[256,1024]{1,0:T(8,128)(2,1)}) %reduce-scatter.23.cloned.1.call-update) | async-done | bytes 524304 | tf_op jit(solution)/shard_map/reduce_scatter | solution.py:178
  260.9 44.7 %all-gather.14.cloned.1.call-done = bf16[1024,1024]{1,0:T(8,128)(2,1)} async-done(((bf16[256,1024]{1,0:T(8,128)(2,1)}), bf16[1024,1024]{1,0:T(8,128)(2,1)}) %all-gather.14.cloned.1.call-update) | async-done | bytes 2097168 | tf_op jit(solution)/shard_map/all_gather | solution.py:187
  305.7 8.5 %convert_reduce_fusion = (f32[1024]{0:T(1024)S(1)}, bf16[1024,1024]{1,0:T(8,128)(2,1)S(1)}) fusion(f32[1024,1024]{1,0:T(8,128)} %get-tuple-element.287, f32[1024,1024]{1,0:T(8,128)} %get-tuple-element.297, f32[1024]{0:T(1024)S(1)} %convert_element_type.190, bf16[1024,1024]{1,0:T(8,128)(2,1)} %all-gather.14.cloned.1.call-done, ...), kind=kOutput, calls=%fused_computation.42 | convolution fusion | flops 2165308416 | bytes 14688256 | tf_op jit(solution)/shard_map/dot_general | solution.py:41
  319.3 5.9 convolution_convert_fusion.1
  329.2 6.0 convolution_convert_fusion.2
  335.5 26.5 %reduce-scatter.25.cloned.1.call-done = bf16[256,1024]{1,0:T(8,128)(2,1)} async-done(((bf16[1024,1024]{1,0:T(8,128)(2,1)}), bf16[256,1024]{1,0:T(8,128)(2,1)}) %reduce-scatter.25.cloned.1.call-update) | async-done | bytes 524304 | tf_op jit(solution)/shard_map/reduce_scatter | solution.py:194
  366.7 13.5 %collective-permute-done = bf16[256,1024]{1,0:T(8,128)(2,1)S(1)} collective-permute-done((bf16[256,1024]{1,0:T(8,128)(2,1)S(1)}, bf16[256,1024]{1,0:T(8,128)(2,1)S(1)}, u32[]{:S(2)}, u32[]{:S(2)}) %collective-permute-start) | collective-permute-done | bytes 524320 | tf_op jit(solution)/shard_map/ppermute | solution.py:16
  383.6 45.5 %collective-permute-done.1 = bf16[512,1024]{1,0:T(8,128)(2,1)} collective-permute-done((bf16[512,1024]{1,0:T(8,128)(2,1)}, bf16[512,1024]{1,0:T(8,128)(2,1)}, u32[]{:S(2)}, u32[]{:S(2)}) %collective-permute-start.1) | collective-permute-done | bytes 1048608 | tf_op jit(solution)/shard_map/ppermute | solution.py:16
  445.4 21.4 %while.28 = (s32[]{:T(128)}, f32[1024,4,64]{0,2,1:T(8,128)S(1)}, f32[1024,4,64]{0,2,1:T(8,128)S(1)}, bf16[2,512,4,64]{1,3,2,0:T(8,128)(2,1)}, bf16[2,512,4,64]{1...) while((s32[]{:T(128)}, f32[1024,4,64]{0,2,1:T(8,128)S(1)}, ...), condition=%wide.region_17.18_spmd.clone, body=%wide.region_15.17_spmd.clone.sunk | while | flops 1362229248 | bytes 76341480 | solution.py:100
  490.9 39.6 %all-reduce = (f32[1024]{0:T(1024)S(1)}, f32[1024]{0:T(1024)S(1)}, f32[1024]{0:T(1024)}, f32[4096]{0:T(1024)S(1)}, f32[1024]{0:T(1024)}, /*index=5*/f32[1024]{0:...) all-reduce(f32[1024]{0:T(1024)S(1)} %bitcast.173, ...), channel_id=1, replica_groups=mesh['dp'=8,'tensor'=4] {'dp','tensor'}, use_global_device_ids=true, to_apply=%region_26.27 | all-reduce | flops 12288 | bytes 98304 | tf_op jit(solution)/shard_map/psum | solution.py:260
  535.7 27.1 %reduce-scatter.33.cloned.1.call-done = bf16[128,256]{1,0:T(8,128)(2,1)} async-done(((bf16[1024,256]{1,0:T(8,128)(2,1)}), bf16[128,256]{1,0:T(8,128)(2,1)}) %reduce-scatter.33.cloned.1.call-update) | async-done | bytes 65552
  564.5 35.3 %reduce-scatter.35.cloned.1.call-done = bf16[128,256]{1,0:T(8,128)(2,1)} async-done(((bf16[1024,256]{1,0:T(8,128)(2,1)}), bf16[128,256]{1,0:T(8,128)(2,1)}) %reduce-scatter.35.cloned.1.call-update) | async-done | bytes 65552
  601.6 44.6 %reduce-scatter.27.cloned.1.call-done = bf16[256,1024]{1,0:T(8,128)(2,1)} async-done(((bf16[1024,1024]{1,0:T(8,128)(2,1)}), bf16[256,1024]{1,0:T(8,128)(2,1)}) %reduce-scatter.27.cloned.1.call-update) | async-done | bytes 524304 | tf_op jit(solution)/shard_map/reduce_scatter | solution.py:222
  (214 shorter events, 128.4 us)
Async XLA Ops:
  8.0 51.1 %all-gather.6.cloned.1.call-start = ((), (), s32[]{:S(2)}) async-start(), calls=%async_computation.10 | async-start | bytes 2621440 | tf_op jit(solution)/shard_map/all_gather | solution.py:152
  8.8 117.2 %reduce-scatter.21.cloned.1.call-start = ((), (), s32[]{:S(2)}) async-start(), calls=%async_computation.11 | async-start | bytes 2621440 | tf_op jit(solution)/shard_map/reduce_scatter | solution.py:164
  21.7 39.7 %copy-start.11 = (bf16[1024,256]{1,0:T(8,128)(2,1)}, bf16[1024,256]{1,0:T(8,128)(2,1)S(1)}, u32[]{:S(2)}) copy-start(bf16[1024,256]{1,0:T(8,128)(2,1)S(1)} %all_gather.28) | copy-start | bytes 1572868
  80.4 45.5 %copy-start = (bf16[256,1024]{1,0:T(8,128)(2,1)S(1)}, bf16[256,1024]{1,0:T(8,128)(2,1)}, u32[]{:S(2)}) copy-start(bf16[256,1024]{1,0:T(8,128)(2,1)} %param.21) | copy-start | bytes 1572868
  81.1 49.7 %copy-start.19 = (bf16[32,8,2,512]{3,1,2,0:T(8,128)(2,1)}, bf16[32,8,2,512]{3,1,2,0:T(8,128)(2,1)S(1)}, u32[]{:S(2)}) copy-start(bf16[32,8,2,512]{3,1,2,0:T(8,128)(2,1)S(1)} %copy.74) | copy-start | bytes 1572868
  83.2 48.4 %copy-start.25 = (bf16[1024]{0:T(1024)(128)(2,1)S(1)}, bf16[1024]{0:T(1024)(128)(2,1)}, u32[]{:S(2)}) copy-start(bf16[1024]{0:T(1024)(128)(2,1)} %param.31) | copy-start | bytes 6148
  83.2 48.5 %all-gather.10.cloned.1.call-start = ((), (), s32[]{:S(2)}) async-start(), calls=%async_computation.13 | async-start | bytes 2359296 | tf_op jit(solution)/shard_map/all_gather | solution.py:148
  83.8 92.0 %all-gather.8.cloned.1.call-start = ((), (), s32[]{:S(2)}) async-start(), calls=%async_computation.12 | async-start | bytes 2621440 | tf_op jit(solution)/shard_map/all_gather | solution.py:174
  130.8 73.7 %all-gather.12.cloned.1.call-start = ((), (), s32[]{:S(2)}) async-start(), calls=%async_computation.14 | async-start | bytes 2359296 | tf_op jit(solution)/shard_map/all_gather | solution.py:149
  131.4 123.1 %reduce-scatter.23.cloned.1.call-start = ((), (), s32[]{:S(2)}) async-start(), calls=%async_computation.15 | async-start | bytes 2621440 | tf_op jit(solution)/shard_map/reduce_scatter | solution.py:178
  204.5 50.0 %copy-start.2 = (bf16[256,1024]{1,0:T(8,128)(2,1)S(1)}, bf16[256,1024]{1,0:T(8,128)(2,1)}, u32[]{:S(2)}) copy-start(bf16[256,1024]{1,0:T(8,128)(2,1)} %reduce-scatter.21.cloned.1.call-done) | copy-start | bytes 1572868
  210.5 45.9 %copy-start.17 = (bf16[256,1024]{1,0:T(8,128)(2,1)S(1)}, bf16[256,1024]{1,0:T(8,128)(2,1)}, u32[]{:S(2)}) copy-start(bf16[256,1024]{1,0:T(8,128)(2,1)} %param.37) | copy-start | bytes 1572868
  210.5 95.2 %all-gather.14.cloned.1.call-start = ((), (), s32[]{:S(2)}) async-start(), calls=%async_computation.16 | async-start | bytes 2621440 | tf_op jit(solution)/shard_map/all_gather | solution.py:187
  260.7 101.4 %reduce-scatter.25.cloned.1.call-start = ((), (), s32[]{:S(2)}) async-start(), calls=%async_computation.17 | async-start | bytes 2621440 | tf_op jit(solution)/shard_map/reduce_scatter | solution.py:194
  319.2 167.4 %reduce-scatter.39.cloned.1.call-start = ((), (), s32[]{:S(2)}) async-start(), calls=%async_computation.24 | async-start | bytes 2359296
  329.2 159.5 %reduce-scatter.29.cloned.1.call-start = ((), (), s32[]{:S(2)}) async-start(), calls=%async_computation.19 | async-start | bytes 2359296 | tf_op jit(solution)/shard_map/reduce_scatter | solution.py:247
  335.2 197.1 %reduce-scatter.37.cloned.1.call-start = ((), (), s32[]{:S(2)}) async-start(), calls=%async_computation.23 | async-start | bytes 589824
  366.7 13.5 %collective-permute-start = (bf16[256,1024]{1,0:T(8,128)(2,1)S(1)}, bf16[256,1024]{1,0:T(8,128)(2,1)S(1)}, u32[]{:S(2)}, u32[]{:S(2)}) collective-permute-start(bf16[256,1024]{1,0:T(8,128)(2,1)S(1)} %get-tuple-element.294), channel_id=1, source_target_pairs={{0,1},{1,0},{2,3},{3,2},{4,5},{5,4},{6,7},{7,6},{8,9},{9,8},{10,11... | collective-permute-start | bytes 1572872 | tf_op jit(solution)/shard_map/ppermute | solution.py:16
  381.7 47.5 %collective-permute-start.1 = (bf16[512,1024]{1,0:T(8,128)(2,1)}, bf16[512,1024]{1,0:T(8,128)(2,1)}, u32[]{:S(2)}, u32[]{:S(2)}) collective-permute-start(bf16[512,1024]{1,0:T(8,128)(2,1)} %maximum_select_fusion.1), channel_id=1, source_target_pairs={{0,2},{1,3},{2,0},{3,1},{4,6},{5,7},{6,4},{7,5},{8,10},{9,11},{10,... | collective-permute-start | bytes 3145736 | tf_op jit(solution)/shard_map/ppermute | solution.py:16
  444.5 89.5 %reduce-scatter.31.cloned.1.call-start = ((), (), s32[]{:S(2)}) async-start(), calls=%async_computation.20 | async-start | bytes 589824
  472.0 90.8 %reduce-scatter.33.cloned.1.call-start = ((), (), s32[]{:S(2)}) async-start(), calls=%async_computation.21 | async-start | bytes 589824
  475.8 124.0 %reduce-scatter.35.cloned.1.call-start = ((), (), s32[]{:S(2)}) async-start(), calls=%async_computation.22 | async-start | bytes 589824
  482.1 164.0 %reduce-scatter.27.cloned.1.call-start = ((), (), s32[]{:S(2)}) async-start(), calls=%async_computation.18 | async-start | bytes 2621440 | tf_op jit(solution)/shard_map/reduce_scatter | solution.py:222
  486.5 159.6 %copy-start.5 = (f32[256,1024]{1,0:T(8,128)S(1)}, f32[256,1024]{1,0:T(8,128)}, u32[]{:S(2)}) copy-start(f32[256,1024]{1,0:T(8,128)} %copy-done.4) | copy-start | bytes 3145732
  (27 other events, 152.2 us)
Sparse Core Ops, SparseCore 0:
  10.4 48.6 all-gather.5
  83.3 42.5 reduce-scatter.20
  210.6 43.8 reduce-scatter.22
  319.4 42.6 reduce-scatter.24
  365.6 40.5 reduce-scatter.38
  409.3 41.2 reduce-scatter.28
  453.9 34.1 reduce-scatter.36
  491.1 34.1 reduce-scatter.30
  528.7 34.0 reduce-scatter.32
  565.7 34.0 reduce-scatter.34
  602.2 43.8 reduce-scatter.26
Sparse Core Ops, SparseCore 1:
  85.7 26.4 all-gather.9
  130.9 44.8 all-gather.7
  177.7 26.8 all-gather.11
  260.7 44.8 all-gather.13
